TPU v7x, 512 devices: a whole 4x8x8 slice. The times are simulated.
512 devices in a mesh: lon: 16 (over z, core), lat: 32 (over y, x).
Axes of the slice: x: 4, y: 8, z: 8, core: 2. Of those that a mesh axis runs over, the one named last changes fastest.
Arguments:
- increment: float32 [2, 64, 768, 2048], P(None, None, 'lat', 'lon'), may hold values from -6 to 6
- eastward_rate: float32 [2, 64, 768], P(None, None, 'lat'), as said below
- eastward_spike: float32 [768, 2048], P('lat', 'lon'), as said below
- northward_rate: float32 [2, 64, 768], replicated, as said below
- vertical: float32 [2, 64, 64], replicated, may hold values from -0.75 to 0.75
Outputs:
- correlated: float32 [2, 64, 768, 2048], P(None, None, 'lat', 'lon')
Inputs may be any that keep to these rules, and one draw needn't show every extreme that they name: `eastward_rate`: every entry is positive and below 1. `eastward_spike`: every entry is positive and at most 1. `northward_rate`: every entry is positive and below 1.
All inputs are finite; a program needn't handle non-finite values.
Results may differ from a plain program's by a relative error of at most 0.0003.
Values sent between devices are 32-bit elements; how exact they have to be, the bound alone decides.
A program may use at most 64 MiB of HBM per device.

v0:
```python
import jax
import jax.numpy as jnp
from jax import lax
from jax.sharding import PartitionSpec as P


def carried_in(x, axis, combine, identity):
    length, mine = (lax.axis_size(axis), lax.axis_index(axis))
    everything = jax.tree.map(lambda part: lax.all_gather(part, axis), x)
    start = jax.tree.map(
        lambda part, zero: jnp.broadcast_to(jnp.asarray(zero, part.dtype), part.shape), x, identity
    )

    def lap(k, before):
        at = length - 1 - k
        reached = at > mine
        new = combine(before, jax.tree.map(lambda part: part[at], everything))
        return jax.tree.map(lambda a, b: jnp.where(reached, a, b), new, before)

    return lax.fori_loop(0, length, lap, start)


def from_root(block, axis, source):
    block = jnp.where(lax.axis_index(axis) == source, block, jnp.zeros_like(block))
    return lax.psum(block, axis)


def compose(earlier, following):
    return (following[0] * earlier[0], following[1] + following[0] * earlier[1])


def matmul_last(values, matrix):
    flat = values.reshape((-1, values.shape[-1]))
    result = jnp.dot(
        flat, matrix, precision=lax.Precision.HIGHEST, preferred_element_type=jnp.float32
    )
    return result.reshape(values.shape[:-1] + (matrix.shape[1],))


def row_filter(rates):
    length = rates.shape[-1]
    totals = jnp.cumsum(jnp.log(rates), axis=-1)
    upper = lax.broadcasted_iota(jnp.int32, (length, length), 0)
    lower = lax.broadcasted_iota(jnp.int32, (length, length), 1)
    keeping = lower <= upper
    spread = totals[..., :, None] - totals[..., None, :]
    weights = jnp.where(keeping, jnp.exp(jnp.where(keeping, spread, -60.0)), 0.0)
    return (weights, jnp.exp(totals))


def shards(increment, eastward_rate, eastward_spike, northward_rate, vertical):
    lon_cols = increment.shape[3]
    decay_factors = eastward_rate[:, :, :, None] * eastward_spike[None, None, :, :]
    row_index = lax.broadcasted_iota(jnp.int32, (lon_cols, lon_cols), 0)
    col_index = lax.broadcasted_iota(jnp.int32, (lon_cols, lon_cols), 1)
    before_mat = (row_index < col_index).astype(jnp.float32)
    suffix_mat = (row_index >= col_index).astype(jnp.float32)
    log_decay = jnp.log(decay_factors)
    prefix_log = matmul_last(log_decay, before_mat)
    total_log = jnp.sum(log_decay, axis=3)
    suffix_sums = matmul_last(jnp.exp(prefix_log) * increment, suffix_mat)
    local_part = jnp.exp(-prefix_log) * suffix_sums
    factor = jnp.exp(total_log[:, :, :, None] - prefix_log)
    block_factor = jnp.exp(total_log)
    block_local = local_part[:, :, :, 0]
    identity_map = (jnp.ones_like(block_factor), jnp.zeros_like(block_local))
    after_factor, after_local = carried_in(
        (block_factor, block_local), "lon", compose, identity_map
    )
    whole_factor, whole_local = compose((after_factor, after_local), (block_factor, block_local))
    shared = from_root(jnp.stack([whole_factor, whole_local]), "lon", 0)
    loop_factor = shared[0]
    loop_local = shared[1]
    wrapped = loop_local / (1.0 - loop_factor)
    incoming = after_local + after_factor * wrapped
    eastward_output = jnp.sqrt(1.0 - decay_factors * decay_factors) * (
        local_part + factor * incoming[:, :, :, None]
    )
    columns = lax.all_to_all(eastward_output, "lat", split_axis=1, concat_axis=2, tiled=True)
    levels_here = columns.shape[1]
    first_level = lax.axis_index("lat") * levels_here
    row_rates = lax.dynamic_slice_in_dim(northward_rate, first_level, levels_here, 1)
    weights, growth = row_filter(row_rates)
    filtered = jnp.einsum("vljk,vlki->vlji", weights, columns, precision=lax.Precision.HIGHEST)
    scaled = jnp.sqrt(1.0 - row_rates * row_rates)[:, :, :, None] * filtered
    meridional_out = lax.all_to_all(scaled, "lat", split_axis=2, concat_axis=1, tiled=True)
    return jnp.einsum("vlk,vlab->vkab", vertical, meridional_out, precision=lax.Precision.HIGHEST)


def solution(mesh):
    return jax.shard_map(
        shards,
        mesh=mesh,
        in_specs=(P(None, None, "lat", "lon"), P(None, None, "lat"), P("lat", "lon"), P(), P()),
        out_specs=P(None, None, "lat", "lon"),
        check_vma=False,
    )
```

profile of v0, /device:TPU:56, one launch (start us, length us, event | category | flops | bytes accessed | tf_op | source)
XLA Modules:
  0.0 214.7 jit_solution(4784289971304212418)
XLA Ops:
  0.0 0.0 copy-start
  0.0 0.0 copy-start.1
  0.0 0.9 copy.57
  0.9 1.7 fusion.12
  2.6 0.0 copy-done.1
  2.6 0.9 fusion.11
  3.5 2.4 %exponential_multiply_fusion = f32[2,64,24,128]{3,2,1,0:T(8,128)S(1)} fusion(f32[2,64,24,128]{3,2,1,0:T(8,128)S(1)} %fusion.12, f32[2,64,24,128]{3,2,1,0:T(8,128)} %param.7), kind=kOutput, calls=%fused_computation.25 | convolution fusion | flops 605175808 | bytes 4718592 | tf_op jit(solution)/shard_map/dot_general | solution.py:34
  6.0 0.5 copy.59
  6.5 25.6 %all-gather.1 = f32[32,64,24,1]{1,2,3,0:T(8,128)} all-gather(f32[2,64,24,1]{1,2,3,0:T(8,128)S(1)} %copy.59), channel_id=3, replica_groups=mesh['lon'=16,'lat'=32] {'lon'}, dimensions={0}, use_global_device_ids=true | all-gather | bytes 208896 | tf_op jit(solution)/shard_map/all_gather | solution.py:9
  32.1 0.1 copy.58
  32.2 16.9 %all-gather = f32[32,64,24]{1,2,0:T(8,128)} all-gather(f32[2,64,24]{1,2,0:T(8,128)S(1)} %exp.29), channel_id=2, replica_groups=mesh['lon'=16,'lat'=32] {'lon'}, dimensions={0}, use_global_device_ids=true | all-gather | bytes 208896 | tf_op jit(solution)/shard_map/all_gather | solution.py:9
  49.2 12.8 %while.18 = (s32[]{:T(128)}, f32[2,64,24]{1,2,0:T(8,128)S(1)}, f32[2,64,24]{1,2,0:T(8,128)S(1)}, s32[]{:T(128)}, f32[16,2,64,24]{2,3,1,0:T(8,128)}, /*index=5*/f...) while((s32[]{:T(128)}, f32[2,64,24]{1,2,0:T(8,128)S(1)}, ...), condition=%wide.region_4.5_spmd.clone, body=%wide.region_3.4_spmd.clone.sunk | while | flops 21512 | bytes 73899 | solution.py:20
  49.2 0.8 fusion.41
  50.0 0.8 fusion.41
  50.8 0.8 fusion.41
  51.6 0.8 fusion.41
  52.4 0.8 fusion.41
  53.2 0.8 fusion.41
  54.0 0.8 fusion.41
  54.8 0.8 fusion.41
  55.6 0.8 fusion.41
  56.4 0.8 fusion.41
  57.2 0.8 fusion.41
  58.0 0.8 fusion.41
  58.8 0.8 fusion.41
  59.6 0.8 fusion.41
  60.4 0.8 fusion.41
  61.2 0.8 fusion.41
  62.0 47.3 %psum.7 = f32[2,2,64,24]{2,3,1,0:T(8,128)S(1)} all-reduce(f32[2,2,64,24]{2,3,1,0:T(8,128)S(1)} %maximum_select_fusion), channel_id=1, replica_groups=mesh['lon'=16,'lat'=32] {'lon'}, use_global_device_ids=true, to_apply=%region_5.6 | all-reduce | flops 6144 | bytes 49152 | tf_op jit(solution)/shard_map/psum | solution.py:25
  109.3 0.1 copy.61
  109.4 1.5 fusion.15
  111.0 1.3 copy.62
  112.2 9.6 %all-to-all-start = ((f32[2,64,24,128]{3,2,0,1:T(8,128)}), f32[2,64,24,128]{3,2,0,1:T(8,128)S(1)}, u32[]{:S(2)}, u32[]{:S(2)}) async-start(f32[2,64,24,128]{3,2,0,1:T(8,128)} %copy.62), calls=%async_computation | async-start | bytes 3145728 | tf_op jit(solution)/shard_map/all_to_all | solution.py:79
  121.8 0.8 subtract_sqrt_fusion
  122.7 1.2 reduce-window.6
  123.8 0.2 slice_reduce_fusion
  124.0 0.4 reduce-window.9
  124.4 0.1 broadcast_add_fusion
  124.5 0.2 iota_compare_fusion
  124.7 30.6 %all-to-all-done = f32[2,64,24,128]{3,2,0,1:T(8,128)S(1)} async-done(((f32[2,64,24,128]{3,2,0,1:T(8,128)}), f32[2,64,24,128]{3,2,0,1:T(8,128)S(1)}, u32[]{:S(2)}, u32[]{:S(2)}) %all-to-all-start) | async-done | bytes 1572896 | tf_op jit(solution)/shard_map/all_to_all | solution.py:79
  155.3 0.1 copy.63
  155.4 10.2 %fusion.21 = f32[2,2,768,128]{3,2,1,0:T(8,128)S(1)} fusion(f32[2,2,768,128]{3,2,1,0:T(8,128)S(1)} %bitcast.62, f32[2,2,768]{2,1,0:T(2,128)S(1)} %reduce_window_sum.23, pred[768,768]{1,0:T(8,128)(4,1)S(1)} %iota_compare_fusion, f32[2,2,768]{2,1,0:T(2,128)S(1)} %get-tuple-element.203), kind=kOutput, calls=%fused_computation.27 | convolution fusion | flops 3631349760 | bytes 3760128 | tf_op jit(solution)/shard_map/vljk,vlki->vlji/dot_general | solution.py:84
  165.6 1.4 copy.64
  167.0 43.2 %all_to_all.36 = f32[2,2,768,128]{3,1,0,2:T(2,128)S(1)} all-to-all(f32[2,2,768,128]{3,1,0,2:T(2,128)S(1)} %copy.64), channel_id=1, replica_groups=mesh['lon'=16,'lat'=32] {'lat'}, dimensions={2} | all-to-all | bytes 3145728 | tf_op jit(solution)/shard_map/all_to_all | solution.py:86
  210.2 0.9 copy.65
  211.1 0.0 copy-done
  211.1 1.5 convolution_bitcast_fusion
  212.6 2.1 copy.67
  (8 shorter events, 0.1 us)
Async XLA Ops:
  0.0 211.1 %copy-start = (f32[2,64,64]{2,1,0:T(8,128)S(1)}, f32[2,64,64]{2,1,0:T(8,128)}, u32[]{:S(2)}) copy-start(f32[2,64,64]{2,1,0:T(8,128)} %param.11) | copy-start | bytes 98308
  0.0 2.6 %copy-start.1 = (f32[24,128]{1,0:T(8,128)S(1)}, f32[24,128]{1,0:T(8,128)}, u32[]{:S(2)}) copy-start(f32[24,128]{1,0:T(8,128)} %param.9) | copy-start | bytes 36868
  112.2 43.1 %all-to-all-start = ((f32[2,64,24,128]{3,2,0,1:T(8,128)}), f32[2,64,24,128]{3,2,0,1:T(8,128)S(1)}, u32[]{:S(2)}, u32[]{:S(2)}) async-start(f32[2,64,24,128]{3,2,0,1:T(8,128)} %copy.62), calls=%async_computation | async-start | bytes 3145728 | tf_op jit(solution)/shard_map/all_to_all | solution.py:79
where the time goes:
time: 219 us; the launch traced here: 215 us
  blocking collectives  133 us (61%)
  waiting for transfers between devices  30.6 us (14%)
  other arithmetic  17.5 us (8%)
  matrix products  15.8 us (7%)
  starting transfers between devices  9.56 us (4%)
  local copies, waits for them, and re-layouts  7.5 us (3%)
    psum x1, blocking collectives, from_root(): return lax.psum(block, axis)  47.3 us
    all_to_all x1, blocking collectives, shards(): lax.all_to_all(scaled, 'lat', split_axis=2, concat_axis=1, tiled=True)  43.2 us
    all_gather x2, blocking collectives, carried_in(): everything = jax.tree.map(lambda part: lax.all_gather(part, axis), x)  42.6 us
    all_to_all x1, waiting for transfers between devices, shards(): lax.all_to_all(eastward_output, 'lat', split_axis=1, concat_axis=2, tiled...  30.6 us
    select_n x16, other arithmetic, lap(): return jax.tree.map(lambda a, b: jnp.where(reached, a, b), new, before)  12.4 us
    dot_general x1, matrix products, shards(): jnp.einsum('vljk,vlki->vlji', weights, columns, precision=lax.Precision.H...  10.2 us
    all_to_all x1, starting transfers between devices, shards(): lax.all_to_all(eastward_output, 'lat', split_axis=1, concat_axis=2, tiled...  9.56 us
  transfers between devices with their start and end apart: 1, of which 1 were waited for; matrix products, arithmetic and copies ran while one was open for 1% of the time, Pallas kernels for 0%

commit v1 on v0

v1 whole, which is shorter than its diff:
```python
import jax
import jax.numpy as jnp
from jax import lax
from jax.experimental import pallas as pl
from jax.experimental.pallas import tpu as pltpu
from jax.sharding import PartitionSpec as P

V, L, J, I = 2, 64, 24, 128
LON, LAT = 16, 32
MESH = pl.DeviceIdType.MESH
f32 = jnp.float32


def lanes(rows):
    return lax.broadcasted_iota(jnp.int32, (rows, I), 1)


def left(x, n):
    size = x.shape[1]
    return pltpu.roll(x, size - n, 1) if n else x


def root(x):
    return x * lax.rsqrt(jnp.maximum(x, 1e-30))


def column(x, j):
    return jnp.broadcast_to(x[:, j : j + 1], (x.shape[0], I))


def pack(nat):
    at = lanes(8)
    out = []
    for h in range(2):
        acc = jnp.zeros((8, I), f32)
        for b in range(8):
            shift = (12 * b - 12 * h) % I
            block = nat[8 * b : 8 * b + 8]
            block = pltpu.roll(block, shift, 1) if shift else block
            acc = jnp.where((at >= 12 * b) & (at < 12 * b + 12), block, acc)
        out.append(acc)
    return out


def unpack(first, second):
    at = lanes(8)
    blocks = []
    for b in range(8):
        one = left(first, 12 * b)
        shift = (12 - 12 * b) % I
        two = pltpu.roll(second, shift, 1) if shift else second
        blocks.append(jnp.where(at < 12, one, jnp.where(at < 24, two, 0.0)))
    return jnp.concatenate(blocks, axis=0)


def kernel(
    x_hbm, er_hbm, sp_hbm, nr_hbm, vert_hbm, out_hbm,
    xin, er, sp, nr, vert, erp, win, suf, sl, sf, wb, gb, ob,
    s1, r1, s2, r2, s3, r3, s4, r4, in_sem, out_sem, send_sem, recv_sem,
):
    e = lax.axis_index("lon")
    q = lax.axis_index("lat")
    ve, vq = e // 8, q // 16

    loads = [
        pltpu.make_async_copy(sp_hbm, sp, in_sem.at[0]),
        pltpu.make_async_copy(er_hbm, er, in_sem.at[1]),
    ]
    for v in range(V):
        for b in range(3):
            n = 3 * v + b
            loads.append(
                pltpu.make_async_copy(x_hbm.at[v, :, pl.ds(8 * b, 8), :], xin.at[n], in_sem.at[2 + n])
            )
    loads.append(pltpu.make_async_copy(nr_hbm, nr, in_sem.at[8]))
    loads.append(pltpu.make_async_copy(vert_hbm, vert, in_sem.at[9]))
    for load in loads:
        load.start()

    barrier = pltpu.get_barrier_semaphore()

    @pl.loop(1, LON)
    def _(t):
        pl.semaphore_signal(barrier, inc=1, device_id={"lon": lax.rem(e + t, LON)}, device_id_type=MESH)

    @pl.loop(1, LAT)
    def _(t):
        pl.semaphore_signal(barrier, inc=1, device_id={"lat": lax.rem(q + t, LAT)}, device_id_type=MESH)

    loads[0].wait()
    spike = sp[...]
    at24 = lanes(J)
    window = jnp.where(at24 < I - 1, spike, 0.0)
    suffix = spike
    for k in range(7):
        win[k] = window
        step = 1 << k
        window = window * left(window, step)
        suffix = suffix * jnp.where(at24 < I - step, left(suffix, step), 1.0)
    suf[...] = suffix
    at1 = lanes(1)
    block_spike = jnp.zeros((1, I), f32)
    for j in range(J):
        block_spike = jnp.where(at1 == j, suffix[j : j + 1, 0:1], block_spike)

    loads[1].wait()
    erp[...] = jnp.zeros_like(erp)
    for v in range(V):
        erp[v, :, 0:J] = er[v]

    at64 = lanes(L)
    xflat = xin.reshape(V * 3 * L * 8, I)
    oflat = ob.reshape(V * 3 * L * 8, I)

    def scan_zonal(v):
        rate = erp[v]
        nat = jnp.zeros((L, I), f32)
        for j in range(J):
            if j % 8 == 0:
                loads[2 + 3 * v + j // 8].wait()
            x = xflat[pl.ds((3 * v + j // 8) * L * 8 + j % 8, L, stride=8), :]
            power = column(rate, j)
            for k in range(7):
                x = x + power * win[k, j : j + 1, :] * left(x, 1 << k)
                power = power * power
            sl[v, j] = x
            nat = jnp.where(at64 == j, pltpu.roll(x, j, 1) if j else x, nat)
        whole = rate
        for k in range(7):
            whole = whole * whole
        whole = whole * block_spike
        for h, part in enumerate(pack(nat)):
            for s in range(8):
                s1[8 * v + s, h : h + 1, :] = part[s : s + 1]
        for h, part in enumerate(pack(whole)):
            for s in range(8):
                s1[8 * v + s, 2 + h : 3 + h, :] = part[s : s + 1]

    def exchange(src, dst, axis, me, size, first, count, send, recv):
        @pl.loop(0, count)
        def _(t):
            to = first + lax.rem(me + t, count)

            @pl.when(to != me)
            def _():
                pltpu.make_async_remote_copy(
                    src_ref=src.at[to], dst_ref=dst.at[me], send_sem=send, recv_sem=recv,
                    device_id={axis: to}, device_id_type=MESH,
                ).start()

            @pl.when(to == me)
            def _():
                pltpu.make_async_copy(src.at[me], dst.at[me], recv).start()

    def wait(ref, first, count, sem):
        part = ref.at[pl.ds(first, count)]
        pltpu.make_async_copy(part, part, sem).wait()

    def scale_zonal(v):
        rate = erp[v]
        logs = jnp.maximum(jnp.log(rate) * 1.4426950408889634, -200.0)
        left_over = (I - at64).astype(f32)
        for j in range(J):
            a = column(rate, j) * sp[j : j + 1, :]
            s = root(1.0 - a * a)
            f = jnp.exp2(column(logs, j) * left_over) * suf[j : j + 1, :]
            sl[v, j] = s * sl[v, j]
            sf[v, j] = s * f

    scan_zonal(0)
    pl.semaphore_wait(barrier, LON + LAT - 2)
    exchange(s1, r1, "lon", e, LON, 0, 8, send_sem.at[0], recv_sem.at[0])
    scan_zonal(1)
    exchange(s1, r1, "lon", e, LON, 8, 8, send_sem.at[0], recv_sem.at[0])
    scale_zonal(0)
    scale_zonal(1)

    wait(r1, 0, LON, recv_sem.at[0])
    total = jnp.zeros((2, I), f32)
    around = jnp.ones((2, I), f32)
    for d in reversed(range(LON)):
        total = r1[d, 0:2, :] + r1[d, 2:4, :] * total
        around = around * r1[d, 2:4, :]
    carry = total / (1.0 - around)
    for d in reversed(range(LON)):
        s2[d] = carry
        carry = r1[d, 0:2, :] + r1[d, 2:4, :] * carry
    exchange(s2, r2, "lon", e, LON, 0, LON, send_sem.at[1], recv_sem.at[1 + ve])

    loads[8].wait()
    start = J * q
    tile, skip = start // I, lax.rem(start, I)
    back = lax.rem(I - skip, I)
    nxt = jnp.minimum(tile + 1, 5)
    north, scale, reach = [], [], []
    for v in range(V):
        one = pltpu.roll(nr[v, :, pl.ds(pl.multiple_of(tile * I, I), I)], back, 1)
        two = pltpu.roll(nr[v, :, pl.ds(pl.multiple_of(nxt * I, I), I)], back, 1)
        rates = jnp.where(at64 < I - skip, one, two)
        north.append(rates)
        s = root(1.0 - rates * rates)
        grown = rates
        for k in range(5):
            step = 1 << k
            grown = grown * jnp.where(at64 >= step, pltpu.roll(grown, step, 1), 1.0)
        scale.append(s)
        reach.append(s * grown)

    rows = nr[vq, pl.ds(pl.multiple_of(8 * (lax.rem(q, 16) // 2), 8), 8), :]
    two = rows * left(rows, 1)
    four = two * left(two, 2)
    eight = four * left(four, 4)
    sixteen = eight * left(eight, 8)
    band = sixteen * left(eight, 16)
    band = jnp.where(lax.rem(q, 2) == 0, band[0:4], band[4:8])
    for d in range(LAT):
        gb[d] = jnp.broadcast_to(band[:, J * d : J * d + 1], (4, I))

    loads[9].wait()
    mats = []
    for v in range(V):
        t = vert[v].T
        hi = t.astype(jnp.bfloat16)
        lo = (t - hi.astype(f32)).astype(jnp.bfloat16)
        mats.append(jnp.concatenate([hi, hi, lo], axis=1))

    def filter_north(v):
        wait(r2, 8 * v, 8, recv_sem.at[1 + v])
        halves = []
        for h in range(2):
            halves.append(jnp.concatenate([r2[8 * v + s, h : h + 1, :] for s in range(8)], axis=0))
        inc = unpack(*halves)
        w = jnp.zeros((L, I), f32)
        for j in range(J):
            w = sl[v, j] + sf[v, j] * column(inc, j) + column(north[v], j) * w
            wb[v, j] = w
        for b in range(16):
            s3[16 * v + b] = w[4 * b : 4 * b + 4]
        exchange(s3, r3, "lat", q, LAT, 16 * v, 16, send_sem.at[2], recv_sem.at[3])

    filter_north(0)
    filter_north(1)
    for v in range(V):
        for j in range(J):
            wb[v, j] = wb[v, j] * column(scale[v], j)

    wait(r3, 0, LAT, recv_sem.at[3])
    carry = jnp.zeros((4, I), f32)
    for d in range(LAT):
        s4[d] = carry
        carry = r3[d] + gb[d] * carry
    exchange(s4, r4, "lat", q, LAT, 0, LAT, send_sem.at[3], recv_sem.at[4 + vq])

    stores = []
    for v in range(V):
        wait(r4, 16 * v, 16, recv_sem.at[4 + v])
        carry = jnp.concatenate([r4[16 * v + b] for b in range(16)], axis=0)
        for j in range(0, J, 2):
            his, los = [], []
            for jj in (j, j + 1):
                m = wb[v, jj] + column(reach[v], jj) * carry
                hi = m.astype(jnp.bfloat16)
                his.append(hi)
                los.append((m - hi.astype(f32)).astype(jnp.bfloat16))
            hi = jnp.concatenate(his, axis=1)
            lo = jnp.concatenate(los, axis=1)
            y = jnp.dot(mats[v], jnp.concatenate([hi, lo, hi], axis=0), preferred_element_type=f32)
            for n, jj in enumerate((j, j + 1)):
                oflat[pl.ds((3 * v + jj // 8) * L * 8 + jj % 8, L, stride=8), :] = y[:, I * n : I * n + I]
            if j % 8 == 6:
                n = 3 * v + j // 8
                store = pltpu.make_async_copy(ob.at[n], out_hbm.at[v, :, pl.ds(8 * (j // 8), 8), :], out_sem.at[n])
                store.start()
                stores.append(store)
    wait(s1, 0, LON - 1, send_sem.at[0])
    wait(s2, 0, LON - 1, send_sem.at[1])
    wait(s3, 0, LAT - 1, send_sem.at[2])
    wait(s4, 0, LAT - 1, send_sem.at[3])
    for store in stores:
        store.wait()


def shards(increment, eastward_rate, eastward_spike, northward_rate, vertical):
    anywhere = pl.BlockSpec(memory_space=pl.ANY)
    vm = pltpu.VMEM
    return pl.pallas_call(
        kernel,
        out_shape=jax.ShapeDtypeStruct((V, L, J, I), f32),
        in_specs=[anywhere] * 5,
        out_specs=anywhere,
        scratch_shapes=[
            vm((V * 3, L, 8, I), f32),
            vm((V, L, J), f32),
            vm((J, I), f32),
            vm((V, L, J * LAT), f32),
            vm((V, L, L), f32),
            vm((V, L, I), f32),
            vm((7, J, I), f32),
            vm((J, I), f32),
            vm((V, J, L, I), f32),
            vm((V, J, L, I), f32),
            vm((V, J, L, I), f32),
            vm((LAT, 4, I), f32),
            vm((V * 3, L, 8, I), f32),
            vm((LON, 4, I), f32),
            vm((LON, 4, I), f32),
            vm((LON, 2, I), f32),
            vm((LON, 2, I), f32),
            vm((LAT, 4, I), f32),
            vm((LAT, 4, I), f32),
            vm((LAT, 4, I), f32),
            vm((LAT, 4, I), f32),
            pltpu.SemaphoreType.DMA((10,)),
            pltpu.SemaphoreType.DMA((6,)),
            pltpu.SemaphoreType.DMA((4,)),
            pltpu.SemaphoreType.DMA((6,)),
        ],
        compiler_params=pltpu.CompilerParams(
            collective_id=0, has_side_effects=True, vmem_limit_bytes=56 * 1024 * 1024
        ),
    )(increment, eastward_rate, eastward_spike, northward_rate, vertical)


def solution(mesh):
    return jax.shard_map(
        shards,
        mesh=mesh,
        in_specs=(P(None, None, "lat", "lon"), P(None, None, "lat"), P("lat", "lon"), P(), P()),
        out_specs=P(None, None, "lat", "lon"),
        check_vma=False,
    )
```

time: 219 us -> 46.6 us (0.21)
  the two profiles are of different devices: /device:TPU:56 before, /device:TPU:8 now
where the time goes in v1:
time: 46.6 us; the launch traced here: 46.4 us
  Pallas kernels  42.3 us (91%)
  local copies, waits for them, and re-layouts  4.1 us (9%)
    pallas_call x1, Pallas kernels, shards(): pl.pallas_call(kernel, out_shape=jax.ShapeDtypeStruct((V, L, J, I), f32),...  42.3 us
    unnamed x2, local copies, waits for them, and re-layouts  4.1 us

profile of v1, /device:TPU:8, one launch (start us, length us, event | category | flops | bytes accessed | tf_op | source)
XLA Modules:
  0.0 46.4 jit_solution(4685820392963801668)
XLA Ops:
  0.0 1.4 %copy.6.er_hbm = f32[2,64,24]{2,1,0:T(8,128)} copy(f32[2,64,24]{1,2,0:T(8,128)} %param.6) | data formatting | bytes 24576 | tf_op args[1]
  1.4 42.3 %shard_map.55 = f32[2,64,24,128]{3,2,1,0:T(8,128)} custom-call(f32[2,64,24,128]{3,2,1,0:T(8,128)} %x_hbm.1, f32[2,64,24]{2,1,0:T(8,128)} %copy.6.er_hbm, f32[24,128]{1,0:T(8,128)} %sp_hbm.1, f32[2,64,768]{2,1,0:T(8,128)} %nr_hbm.1, f32[2,64,64]{2,1,0:T(8,128)} %vert_hbm.1), custom_call_target="tpu_custom_call" | custom-call | tf_op jit(solution)/shard_map/pallas_call | solution.py:286
  43.8 2.7 %copy.8 = f32[2,64,24,128]{3,2,1,0:T(8,128)} copy(f32[2,64,24,128]{3,2,1,0:T(8,128)} %shard_map.55) | data formatting | bytes 3145728

commit v2 on v1

v2 whole, which is shorter than its diff:
```python
import jax
import jax.numpy as jnp
from jax import lax
from jax.experimental import pallas as pl
from jax.experimental.pallas import tpu as pltpu
from jax.sharding import PartitionSpec as P

V, L, J, I = 2, 64, 24, 128
LON, LAT = 16, 32
MESH = pl.DeviceIdType.MESH
f32 = jnp.float32


def lanes(rows):
    return lax.broadcasted_iota(jnp.int32, (rows, I), 1)


def left(x, n):
    size = x.shape[1]
    return pltpu.roll(x, size - n, 1) if n else x


def root(x):
    return x * lax.rsqrt(jnp.maximum(x, 1e-30))


def column(x, j):
    return jnp.broadcast_to(x[:, j : j + 1], (x.shape[0], I))


def pack(nat):
    at = lanes(8)
    out = []
    for h in range(2):
        acc = jnp.zeros((8, I), f32)
        for b in range(8):
            shift = (12 * b - 12 * h) % I
            block = nat[8 * b : 8 * b + 8]
            block = pltpu.roll(block, shift, 1) if shift else block
            acc = jnp.where((at >= 12 * b) & (at < 12 * b + 12), block, acc)
        out.append(acc)
    return out


def unpack(first, second):
    at = lanes(8)
    blocks = []
    for b in range(8):
        one = left(first, 12 * b)
        shift = (12 - 12 * b) % I
        two = pltpu.roll(second, shift, 1) if shift else second
        blocks.append(jnp.where(at < 12, one, jnp.where(at < 24, two, 0.0)))
    return jnp.concatenate(blocks, axis=0)


def kernel(
    x_hbm, er_hbm, sp_hbm, nr_hbm, vert_hbm, wb, inflow, extent, mixing,
    xin, er, sp, nr, vert, erp, win, suf, sl, sf, nb, gb, part, power,
    spikes, ends, s3, r3, s4, r4, in_sem, send_sem, recv_sem,
):
    e = lax.axis_index("lon")
    q = lax.axis_index("lat")
    vq = q // 16

    loads = [
        pltpu.make_async_copy(sp_hbm, sp, in_sem.at[0]),
        pltpu.make_async_copy(er_hbm, er, in_sem.at[1]),
    ]
    for v in range(V):
        for b in range(3):
            n = 3 * v + b
            loads.append(
                pltpu.make_async_copy(x_hbm.at[v, :, pl.ds(8 * b, 8), :], xin.at[n], in_sem.at[2 + n])
            )
    loads.append(pltpu.make_async_copy(nr_hbm, nr, in_sem.at[8]))
    loads.append(pltpu.make_async_copy(vert_hbm, vert, in_sem.at[9]))
    for load in loads:
        load.start()

    barrier = pltpu.get_barrier_semaphore()

    @pl.loop(1, LAT)
    def _(t):
        pl.semaphore_signal(barrier, inc=1, device_id={"lat": lax.rem(q + t, LAT)}, device_id_type=MESH)

    @pl.loop(1, LON)
    def _(t):
        pl.semaphore_signal(barrier, inc=1, device_id={"lon": lax.rem(e + t, LON)}, device_id_type=MESH)

    loads[0].wait()
    spike = sp[...]
    at24 = lanes(J)
    window = jnp.where(at24 < I - 1, spike, 0.0)
    suffix = spike
    for k in range(7):
        win[k] = window
        step = 1 << k
        window = window * left(window, step)
        suffix = suffix * jnp.where(at24 < I - step, left(suffix, step), 1.0)
    suf[...] = suffix
    at1 = lanes(1)
    for h in range(2):
        row = jnp.zeros((1, I), f32)
        for j in range(12):
            own = (lax.rem(at1, 12) == j) & (at1 < 96)
            row = jnp.where(own, suffix[12 * h + j : 12 * h + j + 1, 0:1], row)
        spikes[e, h : h + 1, :] = row

    loads[1].wait()
    erp[...] = jnp.zeros_like(erp)
    for v in range(V):
        erp[v, :, 0:J] = er[v].T

    at64 = lanes(L)
    left_over = (I - at64).astype(f32)
    xflat = xin.reshape(V * 3 * L * 8, I)

    def scan_zonal(v):
        def rows(b, nat):
            n = 3 * v + b
            pltpu.make_async_copy(x_hbm.at[v, :, pl.ds(8 * b, 8), :], xin.at[n], in_sem.at[2 + n]).wait()
            rate = pltpu.roll(erp[v], lax.rem(I - 8 * b, I), 1)
            for k in range(7):
                for jj in range(8):
                    if k == 0:
                        x = xflat[pl.ds(n * L * 8 + jj, L, stride=8), :]
                        p = column(rate, jj)
                    else:
                        x = part[jj]
                        p = power[jj]
                        p = p * p
                    x = x + p * win[k, pl.ds(8 * b + jj, 1), :] * left(x, 1 << k)
                    if k < 6:
                        power[jj] = p
                        part[jj] = x
                    else:
                        sl[v, 8 * b + jj] = x
                        nat = jnp.where(at64 == 8 * b + jj, jnp.broadcast_to(x[:, 0:1], (L, I)), nat)
            return nat

        nat = lax.fori_loop(0, 3, rows, jnp.zeros((L, I), f32))
        for h, tile in enumerate(pack(nat)):
            ends[e, v, h] = tile

    def spread(ref, of, send, recv):
        @pl.loop(1, LON)
        def _(t):
            mine = of(ref.at[e])
            pltpu.make_async_remote_copy(
                src_ref=mine, dst_ref=mine, send_sem=send, recv_sem=recv,
                device_id={"lon": lax.rem(e + t, LON)}, device_id_type=MESH,
            ).start()

    def exchange(src, dst, axis, me, size, first, count, send, recv):
        @pl.loop(0, count)
        def _(t):
            to = first + lax.rem(me + t, count)

            @pl.when(to != me)
            def _():
                pltpu.make_async_remote_copy(
                    src_ref=src.at[to], dst_ref=dst.at[me], send_sem=send, recv_sem=recv,
                    device_id={axis: to}, device_id_type=MESH,
                ).start()

            @pl.when(to == me)
            def _():
                pltpu.make_async_copy(src.at[me], dst.at[me], recv).start()

    def wait(ref, sem):
        pltpu.make_async_copy(ref, ref, sem).wait()

    scan_zonal(0)
    pl.semaphore_wait(barrier, LON + LAT - 2)
    spread(ends, lambda r: r.at[0], send_sem.at[1], recv_sem.at[1])
    spread(spikes, lambda r: r, send_sem.at[0], recv_sem.at[0])
    scan_zonal(1)
    spread(ends, lambda r: r.at[1], send_sem.at[2], recv_sem.at[2])

    loads[8].wait()
    start = J * q
    tile, skip = start // I, lax.rem(start, I)
    back = lax.rem(I - skip, I)
    nxt = jnp.minimum(tile + 1, 5)
    north, scale, reach, onward = [], [], [], []
    for v in range(V):
        one = pltpu.roll(nr[v, :, pl.ds(pl.multiple_of(tile * I, I), I)], back, 1)
        two = pltpu.roll(nr[v, :, pl.ds(pl.multiple_of(nxt * I, I), I)], back, 1)
        rates = jnp.where(at64 < I - skip, one, two)
        north.append(rates)
        s = root(1.0 - rates * rates)
        grown = rates
        for k in range(5):
            step = 1 << k
            grown = grown * jnp.where(at64 >= step, pltpu.roll(grown, step, 1), 1.0)
        scale.append(s)
        reach.append(s * grown)
        after = jnp.where(at64 < J - 1, left(rates, 1), 1.0)
        for k in range(5):
            after = after * left(after, 1 << k)
        onward.append(after)

    early = []
    for v in range(V):
        rate = erp[v]
        logs = jnp.maximum(jnp.log(rate) * 1.4426950408889634, -200.0)
        acc = jnp.zeros((L, I), f32)
        for j in range(J):
            a = column(rate, j) * sp[j : j + 1, :]
            s = root(1.0 - a * a)
            f = jnp.exp2(column(logs, j) * left_over) * suf[j : j + 1, :]
            x = s * sl[v, j]
            n = column(north[v], j)
            sl[v, j] = x
            sf[v, j] = s * f
            nb[v, j] = n
            acc = x + n * acc
        early.append(acc)

    rows = nr[vq, pl.ds(pl.multiple_of(8 * (lax.rem(q, 16) // 2), 8), 8), :]
    two = rows * left(rows, 1)
    four = two * left(two, 2)
    eight = four * left(four, 4)
    sixteen = eight * left(eight, 8)
    band = sixteen * left(eight, 16)
    band = jnp.where(lax.rem(q, 2) == 0, band[0:4], band[4:8])
    for d in range(LAT):
        gb[d] = jnp.broadcast_to(band[:, J * d : J * d + 1], (4, I))

    loads[9].wait()
    for v in range(V):
        t = vert[v].T
        hi = t.astype(jnp.bfloat16)
        lo = (t - hi.astype(f32)).astype(jnp.bfloat16)
        mixing[v] = jnp.concatenate([hi, hi, lo], axis=1)
        extent[v] = reach[v]

    wholes = []
    for v in range(V):
        whole = erp[v]
        for k in range(7):
            whole = whole * whole
        wholes.append(pack(whole))

    incoming = []
    for v in range(V):
        if v == 0:
            wait(spikes.at[pl.ds(0, LON - 1)], recv_sem.at[0])
        wait(ends.at[pl.ds(0, LON - 1), v], recv_sem.at[1 + v])
        halves = []
        for h in range(2):
            total = jnp.zeros((8, I), f32)
            around = jnp.ones((8, I), f32)
            for d in reversed(range(1, LON + 1)):
                at = lax.rem(e + d, LON)
                factor = wholes[v][h] * spikes[at, h : h + 1, :]
                total = ends[at, v, h] + factor * total
                around = around * factor
            halves.append(total / (1.0 - around))
        inc = unpack(*halves)
        incoming.append(inc)
        push = inc * onward[v]
        acc = early[v]
        for j in range(J):
            acc = acc + sf[v, j] * column(push, j)
        for b in range(16):
            s3[16 * v + b] = acc[4 * b : 4 * b + 4]
        exchange(s3, r3, "lat", q, LAT, 16 * v, 16, send_sem.at[3], recv_sem.at[3])

    for v in range(V):
        w = jnp.zeros((L, I), f32)
        for j in range(J):
            w = sl[v, j] + sf[v, j] * column(incoming[v], j) + nb[v, j] * w
            wb[v, j] = w * column(scale[v], j)

    wait(r3, recv_sem.at[3])
    carry = jnp.zeros((4, I), f32)
    for d in range(LAT):
        s4[d] = carry
        carry = r3[d] + gb[d] * carry
    exchange(s4, r4, "lat", q, LAT, 0, LAT, send_sem.at[4], recv_sem.at[4 + vq])

    for v in range(V):
        wait(r4.at[pl.ds(16 * v, 16)], recv_sem.at[4 + v])
        for b in range(16):
            inflow[v, 4 * b : 4 * b + 4] = r4[16 * v + b]
    wait(spikes.at[pl.ds(0, LON - 1)], send_sem.at[0])
    wait(ends.at[pl.ds(0, LON - 1), 0], send_sem.at[1])
    wait(ends.at[pl.ds(0, LON - 1), 1], send_sem.at[2])
    wait(s3.at[pl.ds(0, LAT - 1)], send_sem.at[3])
    wait(s4.at[pl.ds(0, LAT - 1)], send_sem.at[4])


def finish(wb, inflow, extent, mixing, out_hbm, ob, out_sem):
    oflat = ob.reshape(V * 3 * L * 8, I)
    stores = []
    for v in range(V):
        carry = inflow[v]
        for j in range(0, J, 2):
            his, los = [], []
            for jj in (j, j + 1):
                m = wb[v, jj] + column(extent[v], jj) * carry
                hi = m.astype(jnp.bfloat16)
                his.append(hi)
                los.append((m - hi.astype(f32)).astype(jnp.bfloat16))
            hi = jnp.concatenate(his, axis=1)
            lo = jnp.concatenate(los, axis=1)
            y = jnp.dot(mixing[v], jnp.concatenate([hi, lo, hi], axis=0), preferred_element_type=f32)
            for n, jj in enumerate((j, j + 1)):
                oflat[pl.ds((3 * v + jj // 8) * L * 8 + jj % 8, L, stride=8), :] = y[:, I * n : I * n + I]
            if j % 8 == 6:
                n = 3 * v + j // 8
                store = pltpu.make_async_copy(ob.at[n], out_hbm.at[v, :, pl.ds(8 * (j // 8), 8), :], out_sem.at[n])
                store.start()
                stores.append(store)
    for store in stores:
        store.wait()


def shards(increment, eastward_rate, eastward_spike, northward_rate, vertical):
    anywhere = pl.BlockSpec(memory_space=pltpu.HBM)
    vm = pltpu.VMEM
    here = pl.BlockSpec(memory_space=pltpu.VMEM)
    held = [
        pltpu.with_memory_space_constraint(a, pltpu.HBM)
        for a in (increment, eastward_rate.transpose(0, 2, 1), eastward_spike, northward_rate, vertical)
    ]
    parts = pl.pallas_call(
        kernel,
        out_shape=[
            vm((V, J, L, I), f32),
            vm((V, L, I), f32),
            vm((V, L, I), f32),
            vm((V, L, 3 * L), jnp.bfloat16),
        ],
        in_specs=[anywhere] * 5,
        out_specs=[here] * 4,
        scratch_shapes=[
            vm((V * 3, L, 8, I), f32),
            vm((V, J, L), f32),
            vm((J, I), f32),
            vm((V, L, J * LAT), f32),
            vm((V, L, L), f32),
            vm((V, L, I), f32),
            vm((7, J, I), f32),
            vm((J, I), f32),
            vm((V, J, L, I), f32),
            vm((V, J, L, I), f32),
            vm((V, J, L, I), f32),
            vm((LAT, 4, I), f32),
            vm((8, L, I), f32),
            vm((8, L, I), f32),
            vm((LON, 2, I), f32),
            vm((LON, V, 2, 8, I), f32),
            vm((LAT, 4, I), f32),
            vm((LAT, 4, I), f32),
            vm((LAT, 4, I), f32),
            vm((LAT, 4, I), f32),
            pltpu.SemaphoreType.DMA((10,)),
            pltpu.SemaphoreType.DMA((5,)),
            pltpu.SemaphoreType.DMA((6,)),
        ],
        compiler_params=pltpu.CompilerParams(
            collective_id=0, has_side_effects=True, vmem_limit_bytes=48 * 1024 * 1024
        ),
    )(*held)
    return pl.pallas_call(
        finish,
        out_shape=jax.ShapeDtypeStruct((V, L, J, I), f32),
        in_specs=[here] * 4,
        out_specs=anywhere,
        scratch_shapes=[vm((V * 3, L, 8, I), f32), pltpu.SemaphoreType.DMA((6,))],
        compiler_params=pltpu.CompilerParams(vmem_limit_bytes=48 * 1024 * 1024),
    )(*parts)


def solution(mesh):
    return jax.shard_map(
        shards,
        mesh=mesh,
        in_specs=(P(None, None, "lat", "lon"), P(None, None, "lat"), P("lat", "lon"), P(), P()),
        out_specs=P(None, None, "lat", "lon"),
        check_vma=False,
    )
```

time: 46.6 us -> 38.5 us (0.83)
  the two profiles are of different devices: /device:TPU:8 before, /device:TPU:1 now
where the time goes in v2:
time: 38.5 us; the launch traced here: 38.3 us
  Pallas kernels  38.3 us (99%)
    pallas_call x1, Pallas kernels, shards(): pl.pallas_call(kernel, out_shape=[vm((V, J, L, I), f32), vm((V, L, I), f3...  36.7 us
    pallas_call x1, Pallas kernels, shards(): pl.pallas_call(finish, out_shape=jax.ShapeDtypeStruct((V, L, J, I), f32),...  1.63 us

profile of v2, /device:TPU:1, one launch (start us, length us, event | category | flops | bytes accessed | tf_op | source)
XLA Modules:
  0.0 38.3 jit_solution(14662190643113065234)
XLA Ops:
  0.0 36.7 %shard_map.55 = (f32[2,24,64,128]{3,2,1,0:T(8,128)S(1)}, f32[2,64,128]{2,1,0:T(8,128)S(1)}, f32[2,64,128]{2,1,0:T(8,128)S(1)}, bf16[2,64,192]{2,1,0:T(8,128)(2,1)S(1)}) custom-call(f32[2,64,24,128]{3,2,1,0:T(8,128)} %x_hbm.1, f32[2,24,64]{2,1,0:T(8,128)} %bitcast.1, f32[24,128]{1,0:T(8,128)} %sp_hbm.1, f32[2,64,768]{2,1,0:T(8,128)} %nr_hbm.1, ...), custom_call_target="tpu_custom_call" | custom-call | tf_op jit(solution)/shard_map/pallas_call | solution.py:328
  36.7 1.6 %shard_map.56 = f32[2,64,24,128]{3,2,1,0:T(8,128)} custom-call(f32[2,24,64,128]{3,2,1,0:T(8,128)S(1)} %get-tuple-element.9.wb, f32[2,64,128]{2,1,0:T(8,128)S(1)} %get-tuple-element.10.inflow, f32[2,64,128]{2,1,0:T(8,128)S(1)} %get-tuple-element.11.extent, bf16[2,64,192]{2,1,0:T(8,128)(2,1)S(1)} %get-tuple-element.12.mixing), custom_call_target="tpu_custom_call" | custom-call | tf_op jit(solution)/shard_map/pallas_call | solution.py:367

commit v3 on v2

v3 whole, which is shorter than its diff:
```python
import jax
import jax.numpy as jnp
from jax import lax
from jax.experimental import pallas as pl
from jax.experimental.pallas import tpu as pltpu
from jax.sharding import PartitionSpec as P

V, L, J, I = 2, 64, 24, 128
LON, LAT = 16, 32
MESH = pl.DeviceIdType.MESH
f32 = jnp.float32


def lanes(rows):
    return lax.broadcasted_iota(jnp.int32, (rows, I), 1)


def left(x, n):
    size = x.shape[1]
    return pltpu.roll(x, size - n, 1) if n else x


def root(x):
    return x * lax.rsqrt(jnp.maximum(x, 1e-30))


def column(x, j):
    return jnp.broadcast_to(x[:, j : j + 1], (x.shape[0], I))


def pack(nats):
    at = lanes(8)
    tiles = [jnp.zeros((8, I), f32)] * 3
    for v in range(V):
        for b in range(8):
            t, c = divmod(8 * J * v + J * b, I)
            block = nats[v][8 * b : 8 * b + 8]
            block = pltpu.roll(block, c, 1) if c else block
            tiles[t] = jnp.where((at >= c) & (at < c + J), block, tiles[t])
            if c + J > I:
                tiles[t + 1] = jnp.where(at < c + J - I, block, tiles[t + 1])
    return tiles


def unpack(tiles, v):
    at = lanes(8)
    blocks = []
    for b in range(8):
        t, c = divmod(8 * J * v + J * b, I)
        block = left(tiles[t], c)
        if c + J > I:
            block = jnp.where(at < I - c, block, left(tiles[t + 1], c))
        blocks.append(jnp.where(at < J, block, 0.0))
    return jnp.concatenate(blocks, axis=0)


def kernel(
    x_hbm, er_hbm, sp_hbm, nr_hbm, vert_hbm, wb, inflow, extent, mixing,
    xin, er, sp, nr, vert, erp, logs, win, pre, suf, sl, sf, nb, gb, part, power,
    scale, onward, early, whole_tiles, spikes, shares, ends, s3, r3, s4, r4, in_sem, send_sem, recv_sem,
):
    e = lax.axis_index("lon")
    q = lax.axis_index("lat")
    vq = q // 16

    loads = [
        pltpu.make_async_copy(sp_hbm, sp, in_sem.at[0]),
        pltpu.make_async_copy(er_hbm, er, in_sem.at[1]),
    ]
    for v in range(V):
        for b in range(3):
            n = 3 * v + b
            loads.append(
                pltpu.make_async_copy(x_hbm.at[v, :, pl.ds(8 * b, 8), :], xin.at[n], in_sem.at[2 + n])
            )
    loads.append(pltpu.make_async_copy(nr_hbm, nr, in_sem.at[8]))
    loads.append(pltpu.make_async_copy(vert_hbm, vert, in_sem.at[9]))
    for load in loads:
        load.start()

    barrier = pltpu.get_barrier_semaphore()

    for t in range(1, LAT):
        pl.semaphore_signal(barrier, inc=1, device_id={"lat": lax.rem(q + t, LAT)}, device_id_type=MESH)

    for t in range(1, LON):
        pl.semaphore_signal(barrier, inc=1, device_id={"lon": lax.rem(e + t, LON)}, device_id_type=MESH)

    loads[0].wait()
    spike = sp[...]
    at24 = lanes(J)
    prefix = jnp.where(at24 >= 1, pltpu.roll(spike, 1, 1), 1.0)
    for k in range(7):
        step = 1 << k
        prefix = prefix * jnp.where(at24 >= step, pltpu.roll(prefix, step, 1), 1.0)
    pre[...] = prefix
    prefix = prefix * spike
    at1 = lax.rem(lanes(1), J)
    row = jnp.zeros((1, I), f32)
    for j in range(J):
        row = jnp.where(at1 == j, prefix[j : j + 1, I - 1 : I], row)
    spikes[e] = row

    loads[1].wait()
    erp[...] = jnp.zeros_like(erp)
    for v in range(V):
        erp[v, :, 0:J] = er[v].T
    for v in range(V):
        logs[v] = jnp.maximum(jnp.log(erp[v]) * 1.4426950408889634, -200.0)

    at64 = lanes(L)
    left_over = (I - at64).astype(f32)
    xflat = xin.reshape(V * 3 * L * 8, I)

    ones = jnp.ones((2 * I, I), jnp.bfloat16)
    along = at64.astype(f32)

    def sum_zonal(v):
        def rows(b, nat):
            n = 3 * v + b
            pltpu.make_async_copy(x_hbm.at[v, :, pl.ds(8 * b, 8), :], xin.at[n], in_sem.at[2 + n]).wait()
            rate = pltpu.roll(logs[v], lax.rem(I - 8 * b, I), 1)
            for jj in range(8):
                x = xflat[pl.ds(n * L * 8 + jj, L, stride=8), :]
                y = x * jnp.exp2(column(rate, jj) * along) * pre[pl.ds(8 * b + jj, 1), :]
                hi = y.astype(jnp.bfloat16)
                lo = (y - hi.astype(f32)).astype(jnp.bfloat16)
                total = jnp.dot(jnp.concatenate([hi, lo], axis=1), ones, preferred_element_type=f32)
                nat = jnp.where(at64 == 8 * b + jj, total, nat)
            return nat

        return lax.fori_loop(0, 3, rows, jnp.zeros((L, I), f32))

    def scan_zonal(v):
        @pl.loop(0, 3)
        def _(b):
            n = 3 * v + b
            rate = pltpu.roll(erp[v], lax.rem(I - 8 * b, I), 1)
            for k in range(7):
                for jj in range(8):
                    if k == 0:
                        x = xflat[pl.ds(n * L * 8 + jj, L, stride=8), :]
                        p = column(rate, jj)
                    else:
                        x = part[jj]
                        p = power[jj]
                        p = p * p
                    x = x + p * win[k, pl.ds(8 * b + jj, 1), :] * left(x, 1 << k)
                    if k < 6:
                        power[jj] = p
                        part[jj] = x
                    else:
                        sl[v, 8 * b + jj] = x

    def spread(ref, send, recv):
        mine = ref.at[e]
        for t in range(LON - 1):
            to = t + (t >= e).astype(jnp.int32)
            pltpu.make_async_remote_copy(
                src_ref=mine, dst_ref=mine, send_sem=send, recv_sem=recv,
                device_id={"lon": to}, device_id_type=MESH,
            ).start()

    def exchange(src, dst, axis, me, size, first, count, send, recv):
        def send_one(t):
            to = first + lax.rem(me + t, count)
            pltpu.make_async_remote_copy(
                src_ref=src.at[to], dst_ref=dst.at[me], send_sem=send, recv_sem=recv,
                device_id={axis: to}, device_id_type=MESH,
            ).start()

        for t in range(1, count):
            send_one(t)
        mine = me // count == first // count

        @pl.when(mine)
        def _():
            pltpu.make_async_copy(src.at[me], dst.at[me], recv).start()

        @pl.when(jnp.logical_not(mine))
        def _():
            send_one(0)

    def wait(ref, sem):
        pltpu.make_async_copy(ref, ref, sem).wait()

    for t, tile in enumerate(pack([sum_zonal(0), sum_zonal(1)])):
        ends[e, t] = tile

    def prepare_first():
        window = jnp.where(at24 < I - 1, spike, 0.0)
        suffix = spike
        for k in range(7):
            win[k] = window
            step = 1 << k
            window = window * left(window, step)
            suffix = suffix * jnp.where(at24 < I - step, left(suffix, step), 1.0)
        suf[...] = suffix

        scan_zonal(0)

    def prepare_second():
        scan_zonal(1)
        loads[8].wait()
        start = J * q
        tile, skip = start // I, lax.rem(start, I)
        back = lax.rem(I - skip, I)
        nxt = jnp.minimum(tile + 1, 5)
        north = []
        for v in range(V):
            one = pltpu.roll(nr[v, :, pl.ds(pl.multiple_of(tile * I, I), I)], back, 1)
            two = pltpu.roll(nr[v, :, pl.ds(pl.multiple_of(nxt * I, I), I)], back, 1)
            rates = jnp.where(at64 < I - skip, one, two)
            north.append(rates)
            s = root(1.0 - rates * rates)
            grown = rates
            for k in range(5):
                step = 1 << k
                grown = grown * jnp.where(at64 >= step, pltpu.roll(grown, step, 1), 1.0)
            scale[v] = s
            extent[v] = s * grown
            after = jnp.where(at64 < J - 1, left(rates, 1), 1.0)
            for k in range(5):
                after = after * left(after, 1 << k)
            onward[v] = after

        for v in range(V):
            rate = erp[v]
            acc = jnp.zeros((L, I), f32)
            for j in range(J):
                a = column(rate, j) * sp[j : j + 1, :]
                s = root(1.0 - a * a)
                f = jnp.exp2(column(logs[v], j) * left_over) * suf[j : j + 1, :]
                x = s * sl[v, j]
                n = column(north[v], j)
                sl[v, j] = x
                sf[v, j] = s * f
                nb[v, j] = n
                acc = x + n * acc
            early[v] = acc

        rows = nr[vq, pl.ds(pl.multiple_of(8 * (lax.rem(q, 16) // 2), 8), 8), :]
        two = rows * left(rows, 1)
        four = two * left(two, 2)
        eight = four * left(four, 4)
        sixteen = eight * left(eight, 8)
        band = sixteen * left(eight, 16)
        band = jnp.where(lax.rem(q, 2) == 0, band[0:4], band[4:8])
        for d in range(LAT):
            gb[d] = jnp.broadcast_to(band[:, J * d : J * d + 1], (4, I))

        loads[9].wait()
        for v in range(V):
            t = vert[v].T
            hi = t.astype(jnp.bfloat16)
            lo = (t - hi.astype(f32)).astype(jnp.bfloat16)
            mixing[v] = jnp.concatenate([hi, hi, lo], axis=1)

        wholes = []
        for v in range(V):
            whole = erp[v]
            for k in range(7):
                whole = whole * whole
            wholes.append(whole)
        for t, tile in enumerate(pack(wholes)):
            whole_tiles[t] = tile

    def open_and_send():
        pl.semaphore_wait(barrier, LON + LAT - 2)
        spread(spikes, send_sem.at[0], recv_sem.at[0])
        spread(ends, send_sem.at[1], recv_sem.at[1])

    @pl.loop(0, 2)
    def _(phase):
        @pl.when(phase == (e >= 8).astype(jnp.int32))
        def _():
            prepare_first()

        @pl.when(phase == (e >= 4).astype(jnp.int32))
        def _():
            prepare_second()

        @pl.when(phase == 0)
        def _():
            open_and_send()

    wait(spikes.at[pl.ds(0, LON - 1)], recv_sem.at[0])
    at16 = lanes(LON)
    share = jnp.concatenate([spikes[d] for d in range(LON)], axis=0)
    shares[0] = share
    shares[1] = jnp.where(at16 < I - 8, left(share, 8), pltpu.roll(share, 16, 1))
    shares[2] = jnp.where(at16 < I - 16, left(share, 16), pltpu.roll(share, 8, 1))
    wait(ends.at[pl.ds(0, LON - 1)], recv_sem.at[1])
    tiles = []
    for t in range(3):
        total = jnp.zeros((8, I), f32)
        around = jnp.ones((8, I), f32)
        for d in reversed(range(1, LON + 1)):
            at = lax.rem(e + d, LON)
            factor = whole_tiles[t] * shares[t, pl.ds(at, 1), :]
            total = ends[at, t] + factor * total
            around = around * factor
        tiles.append(total / (1.0 - around))
    incoming = []
    for v in range(V):
        inc = unpack(tiles, v)
        incoming.append(inc)
        push = inc * onward[v]
        acc = early[v]
        for j in range(J):
            acc = acc + sf[v, j] * column(push, j)
        for b in range(16):
            s3[16 * v + b] = acc[4 * b : 4 * b + 4]
        exchange(s3, r3, "lat", q, LAT, 16 * v, 16, send_sem.at[3], recv_sem.at[3])

    for v in range(V):
        w = jnp.zeros((L, I), f32)
        for j in range(J):
            w = sl[v, j] + sf[v, j] * column(incoming[v], j) + nb[v, j] * w
            wb[v, j] = w * column(scale[v], j)

    wait(r3, recv_sem.at[3])
    carry = jnp.zeros((4, I), f32)
    for d in range(LAT):
        s4[d] = carry
        carry = r3[d] + gb[d] * carry
    pltpu.make_async_copy(s4.at[q], r4.at[q], recv_sem.at[4 + vq]).start()
    for t in range(LAT - 1):
        to = t + (t >= q).astype(jnp.int32)
        pltpu.make_async_remote_copy(
            src_ref=s4.at[to], dst_ref=r4.at[q], send_sem=send_sem.at[4], recv_sem=recv_sem.at[4 + vq],
            device_id={"lat": to}, device_id_type=MESH,
        ).start()

    for v in range(V):
        wait(r4.at[pl.ds(16 * v, 16)], recv_sem.at[4 + v])
        for b in range(16):
            inflow[v, 4 * b : 4 * b + 4] = r4[16 * v + b]
    wait(spikes.at[pl.ds(0, LON - 1)], send_sem.at[0])
    wait(ends.at[pl.ds(0, LON - 1)], send_sem.at[1])
    wait(s3.at[pl.ds(0, LAT - 1)], send_sem.at[3])
    wait(s4.at[pl.ds(0, LAT - 1)], send_sem.at[4])


def finish(wb, inflow, extent, mixing, out_hbm, ob, out_sem):
    oflat = ob.reshape(V * 3 * L * 8, I)
    stores = []
    for v in range(V):
        carry = inflow[v]
        for j in range(0, J, 2):
            his, los = [], []
            for jj in (j, j + 1):
                m = wb[v, jj] + column(extent[v], jj) * carry
                hi = m.astype(jnp.bfloat16)
                his.append(hi)
                los.append((m - hi.astype(f32)).astype(jnp.bfloat16))
            hi = jnp.concatenate(his, axis=1)
            lo = jnp.concatenate(los, axis=1)
            y = jnp.dot(mixing[v], jnp.concatenate([hi, lo, hi], axis=0), preferred_element_type=f32)
            for n, jj in enumerate((j, j + 1)):
                oflat[pl.ds((3 * v + jj // 8) * L * 8 + jj % 8, L, stride=8), :] = y[:, I * n : I * n + I]
            if j % 8 == 6:
                n = 3 * v + j // 8
                store = pltpu.make_async_copy(ob.at[n], out_hbm.at[v, :, pl.ds(8 * (j // 8), 8), :], out_sem.at[n])
                store.start()
                stores.append(store)
    for store in stores:
        store.wait()


def shards(increment, eastward_rate, eastward_spike, northward_rate, vertical):
    anywhere = pl.BlockSpec(memory_space=pltpu.HBM)
    vm = pltpu.VMEM
    here = pl.BlockSpec(memory_space=pltpu.VMEM)
    held = [
        pltpu.with_memory_space_constraint(a, pltpu.HBM)
        for a in (increment, eastward_rate.transpose(0, 2, 1), eastward_spike, northward_rate, vertical)
    ]
    parts = pl.pallas_call(
        kernel,
        out_shape=[
            vm((V, J, L, I), f32),
            vm((V, L, I), f32),
            vm((V, L, I), f32),
            vm((V, L, 3 * L), jnp.bfloat16),
        ],
        in_specs=[anywhere] * 5,
        out_specs=[here] * 4,
        scratch_shapes=[
            vm((V * 3, L, 8, I), f32),
            vm((V, J, L), f32),
            vm((J, I), f32),
            vm((V, L, J * LAT), f32),
            vm((V, L, L), f32),
            vm((V, L, I), f32),
            vm((V, L, I), f32),
            vm((7, J, I), f32),
            vm((J, I), f32),
            vm((J, I), f32),
            vm((V, J, L, I), f32),
            vm((V, J, L, I), f32),
            vm((V, J, L, I), f32),
            vm((LAT, 4, I), f32),
            vm((8, L, I), f32),
            vm((8, L, I), f32),
            vm((V, L, I), f32),
            vm((V, L, I), f32),
            vm((V, L, I), f32),
            vm((3, 8, I), f32),
            vm((LON, 1, I), f32),
            vm((3, LON, I), f32),
            vm((LON, 3, 8, I), f32),
            vm((LAT, 4, I), f32),
            vm((LAT, 4, I), f32),
            vm((LAT, 4, I), f32),
            vm((LAT, 4, I), f32),
            pltpu.SemaphoreType.DMA((10,)),
            pltpu.SemaphoreType.DMA((5,)),
            pltpu.SemaphoreType.DMA((6,)),
        ],
        compiler_params=pltpu.CompilerParams(
            collective_id=0, has_side_effects=True, vmem_limit_bytes=48 * 1024 * 1024
        ),
    )(*held)
    return pl.pallas_call(
        finish,
        out_shape=jax.ShapeDtypeStruct((V, L, J, I), f32),
        in_specs=[here] * 4,
        out_specs=anywhere,
        scratch_shapes=[vm((V * 3, L, 8, I), f32), pltpu.SemaphoreType.DMA((6,))],
        compiler_params=pltpu.CompilerParams(vmem_limit_bytes=48 * 1024 * 1024),
    )(*parts)


def solution(mesh):
    return jax.shard_map(
        shards,
        mesh=mesh,
        in_specs=(P(None, None, "lat", "lon"), P(None, None, "lat"), P("lat", "lon"), P(), P()),
        out_specs=P(None, None, "lat", "lon"),
        check_vma=False,
    )
```

time: 38.5 us -> 35.8 us (0.930)
  the two profiles are of different devices: /device:TPU:1 before, /device:TPU:64 now
where the time goes in v3:
time: 35.8 us; the launch traced here: 35.6 us
  Pallas kernels  35.6 us (99%)
    pallas_call x1, Pallas kernels, shards(): pl.pallas_call(kernel, out_shape=[vm((V, J, L, I), f32), vm((V, L, I), f3...  34 us
    pallas_call x1, Pallas kernels, shards(): pl.pallas_call(finish, out_shape=jax.ShapeDtypeStruct((V, L, J, I), f32),...  1.63 us

profile of v3, /device:TPU:64, one launch (start us, length us, event | category | flops | bytes accessed | tf_op | source)
XLA Modules:
  0.0 35.6 jit_solution(3700857056352899685)
XLA Ops:
  0.0 34.0 %shard_map.55 = (f32[2,24,64,128]{3,2,1,0:T(8,128)S(1)}, f32[2,64,128]{2,1,0:T(8,128)S(1)}, f32[2,64,128]{2,1,0:T(8,128)S(1)}, bf16[2,64,192]{2,1,0:T(8,128)(2,1)S(1)}) custom-call(f32[2,64,24,128]{3,2,1,0:T(8,128)} %x_hbm.1, f32[2,24,64]{2,1,0:T(8,128)} %bitcast.1, f32[24,128]{1,0:T(8,128)} %sp_hbm.1, f32[2,64,768]{2,1,0:T(8,128)} %nr_hbm.1, ...), custom_call_target="tpu_custom_call" | custom-call | tf_op jit(solution)/shard_map/pallas_call | solution.py:379
  34.0 1.6 %shard_map.56 = f32[2,64,24,128]{3,2,1,0:T(8,128)} custom-call(f32[2,24,64,128]{3,2,1,0:T(8,128)S(1)} %get-tuple-element.9.wb, f32[2,64,128]{2,1,0:T(8,128)S(1)} %get-tuple-element.10.inflow, f32[2,64,128]{2,1,0:T(8,128)S(1)} %get-tuple-element.11.extent, bf16[2,64,192]{2,1,0:T(8,128)(2,1)S(1)} %get-tuple-element.12.mixing), custom_call_target="tpu_custom_call" | custom-call | tf_op jit(solution)/shard_map/pallas_call | solution.py:425

commit v4 on v3

--- a/solution.py
+++ b/solution.py
@@ -6,7 +6,9 @@
 from jax.sharding import PartitionSpec as P
 
 V, L, J, I = 2, 64, 24, 128
+Q = V * L // 4
 LON, LAT = 16, 32
+ROW, ROWS = 4, 8
 MESH = pl.DeviceIdType.MESH
 f32 = jnp.float32
 
@@ -56,12 +58,13 @@
 
 def kernel(
     x_hbm, er_hbm, sp_hbm, nr_hbm, vert_hbm, wb, inflow, extent, mixing,
-    xin, er, sp, nr, vert, erp, logs, win, pre, suf, sl, sf, nb, gb, part, power,
-    scale, onward, early, whole_tiles, spikes, shares, ends, s3, r3, s4, r4, in_sem, send_sem, recv_sem,
+    xin, er, sp, nr, vert, erp, logs, win, pre, suf, sl, sf, nb, gb, gt, part, power,
+    scale, onward, early, whole_tiles, spikes, shares, ends, s3, r3, st, rt, inside, s4, r4,
+    in_sem, send_sem, recv_sem, row_send, row_recv,
 ):
     e = lax.axis_index("lon")
     q = lax.axis_index("lat")
-    vq = q // 16
+    row, col = q // ROW, lax.rem(q, ROW)
 
     loads = [
         pltpu.make_async_copy(sp_hbm, sp, in_sem.at[0]),
@@ -80,11 +83,15 @@
 
     barrier = pltpu.get_barrier_semaphore()
 
-    for t in range(1, LAT):
-        pl.semaphore_signal(barrier, inc=1, device_id={"lat": lax.rem(q + t, LAT)}, device_id_type=MESH)
-
     for t in range(1, LON):
-        pl.semaphore_signal(barrier, inc=1, device_id={"lon": lax.rem(e + t, LON)}, device_id_type=MESH)
+        to = lax.rem(e + t, LON)
+        pl.semaphore_signal(barrier, inc=1, device_id={"lon": to}, device_id_type=MESH)
+    for t in range(1, ROWS):
+        to = lax.rem(row + t, ROWS) * ROW + col
+        pl.semaphore_signal(barrier, inc=1, device_id={"lat": to}, device_id_type=MESH)
+    for t in range(1, ROW):
+        to = row * ROW + lax.rem(col + t, ROW)
+        pl.semaphore_signal(barrier, inc=1, device_id={"lat": to}, device_id_type=MESH)
 
     loads[0].wait()
     spike = sp[...]
@@ -96,10 +103,10 @@
     pre[...] = prefix
     prefix = prefix * spike
     at1 = lax.rem(lanes(1), J)
-    row = jnp.zeros((1, I), f32)
+    periodic = jnp.zeros((1, I), f32)
     for j in range(J):
-        row = jnp.where(at1 == j, prefix[j : j + 1, I - 1 : I], row)
-    spikes[e] = row
+        periodic = jnp.where(at1 == j, prefix[j : j + 1, I - 1 : I], periodic)
+    spikes[e] = periodic
 
     loads[1].wait()
     erp[...] = jnp.zeros_like(erp)
@@ -161,25 +168,17 @@
                 device_id={"lon": to}, device_id_type=MESH,
             ).start()
 
-    def exchange(src, dst, axis, me, size, first, count, send, recv):
-        def send_one(t):
-            to = first + lax.rem(me + t, count)
+    def along_row(src, dst, quarter, to, send, recv):
+        @pl.when(to == col)
+        def _():
+            pltpu.make_async_copy(src.at[quarter], dst.at[col], recv).start()
+
+        @pl.when(to != col)
+        def _():
             pltpu.make_async_remote_copy(
-                src_ref=src.at[to], dst_ref=dst.at[me], send_sem=send, recv_sem=recv,
-                device_id={axis: to}, device_id_type=MESH,
+                src_ref=src.at[quarter], dst_ref=dst.at[col], send_sem=send, recv_sem=recv,
+                device_id={"lat": row * ROW + to}, device_id_type=MESH,
             ).start()
-
-        for t in range(1, count):
-            send_one(t)
-        mine = me // count == first // count
-
-        @pl.when(mine)
-        def _():
-            pltpu.make_async_copy(src.at[me], dst.at[me], recv).start()
-
-        @pl.when(jnp.logical_not(mine))
-        def _():
-            send_one(0)
 
     def wait(ref, sem):
         pltpu.make_async_copy(ref, ref, sem).wait()
@@ -239,15 +238,20 @@
                 acc = x + n * acc
             early[v] = acc
 
-        rows = nr[vq, pl.ds(pl.multiple_of(8 * (lax.rem(q, 16) // 2), 8), 8), :]
+        rows = nr[col // 2, pl.ds(pl.multiple_of(Q * lax.rem(col, 2), Q), Q), :]
         two = rows * left(rows, 1)
         four = two * left(two, 2)
         eight = four * left(four, 4)
         sixteen = eight * left(eight, 8)
         band = sixteen * left(eight, 16)
-        band = jnp.where(lax.rem(q, 2) == 0, band[0:4], band[4:8])
-        for d in range(LAT):
-            gb[d] = jnp.broadcast_to(band[:, J * d : J * d + 1], (4, I))
+        for r in range(ROWS):
+            whole = jnp.ones((Q, I), f32)
+            for c in range(ROW):
+                d = ROW * r + c
+                g = jnp.broadcast_to(band[:, J * d : J * d + 1], (Q, I))
+                gb[d] = g
+                whole = whole * g
+            gt[r] = whole
 
         loads[9].wait()
         for v in range(V):
@@ -266,7 +270,7 @@
             whole_tiles[t] = tile
 
     def open_and_send():
-        pl.semaphore_wait(barrier, LON + LAT - 2)
+        pl.semaphore_wait(barrier, LON + ROWS + ROW - 3)
         spread(spikes, send_sem.at[0], recv_sem.at[0])
         spread(ends, send_sem.at[1], recv_sem.at[1])
 
@@ -309,37 +313,60 @@
         acc = early[v]
         for j in range(J):
             acc = acc + sf[v, j] * column(push, j)
-        for b in range(16):
-            s3[16 * v + b] = acc[4 * b : 4 * b + 4]
-        exchange(s3, r3, "lat", q, LAT, 16 * v, 16, send_sem.at[3], recv_sem.at[3])
-
-    for v in range(V):
+        for h in range(2):
+            s3[2 * v + h] = acc[Q * h : Q * h + Q]
+            along_row(s3, r3, 2 * v + h, 2 * v + h, send_sem.at[2], recv_sem.at[2])
+
+    wait(r3, recv_sem.at[2])
+    total = r3[0]
+    for c in range(1, ROW):
+        total = r3[c] + gb[ROW * row + c] * total
+    st[...] = total
+    for t in range(1, ROWS):
+
+        @pl.when(row + t < ROWS)
+        def _():
+            pltpu.make_async_remote_copy(
+                src_ref=st, dst_ref=rt.at[row], send_sem=row_send.at[t], recv_sem=row_recv.at[row],
+                device_id={"lat": (row + t) * ROW + col}, device_id_type=MESH,
+            ).start()
+
+    def recurse(v):
         w = jnp.zeros((L, I), f32)
         for j in range(J):
             w = sl[v, j] + sf[v, j] * column(incoming[v], j) + nb[v, j] * w
             wb[v, j] = w * column(scale[v], j)
 
-    wait(r3, recv_sem.at[3])
-    carry = jnp.zeros((4, I), f32)
-    for d in range(LAT):
-        s4[d] = carry
-        carry = r3[d] + gb[d] * carry
-    pltpu.make_async_copy(s4.at[q], r4.at[q], recv_sem.at[4 + vq]).start()
-    for t in range(LAT - 1):
-        to = t + (t >= q).astype(jnp.int32)
-        pltpu.make_async_remote_copy(
-            src_ref=s4.at[to], dst_ref=r4.at[q], send_sem=send_sem.at[4], recv_sem=recv_sem.at[4 + vq],
-            device_id={"lat": to}, device_id_type=MESH,
-        ).start()
-
-    for v in range(V):
-        wait(r4.at[pl.ds(16 * v, 16)], recv_sem.at[4 + v])
-        for b in range(16):
-            inflow[v, 4 * b : 4 * b + 4] = r4[16 * v + b]
+    recurse(0)
+    inside[...] = jnp.zeros_like(inside)
+    for r in range(ROWS - 1):
+
+        @pl.when(r < row)
+        def _():
+            pltpu.make_async_copy(rt.at[r], rt.at[r], row_recv.at[r]).wait()
+            inside[...] = rt[r] + gt[r] * inside[...]
+
+    carry = inside[...]
+    for c in range(ROW):
+        s4[c] = carry
+        along_row(s4, r4, c, c, send_sem.at[3], recv_sem.at[3])
+        if c + 1 < ROW:
+            carry = r3[c] + gb[ROW * row + c] * carry
+    recurse(1)
+    wait(r4, recv_sem.at[3])
+    for v in range(V):
+        for h in range(2):
+            inflow[v, Q * h : Q * h + Q] = r4[2 * v + h]
+    for t in range(1, ROWS):
+
+        @pl.when(row + t < ROWS)
+        def _():
+            pltpu.make_async_copy(st, st, row_send.at[t]).wait()
+
     wait(spikes.at[pl.ds(0, LON - 1)], send_sem.at[0])
     wait(ends.at[pl.ds(0, LON - 1)], send_sem.at[1])
-    wait(s3.at[pl.ds(0, LAT - 1)], send_sem.at[3])
-    wait(s4.at[pl.ds(0, LAT - 1)], send_sem.at[4])
+    wait(s3.at[pl.ds(0, ROW - 1)], send_sem.at[2])
+    wait(s4.at[pl.ds(0, ROW - 1)], send_sem.at[3])
 
 
 def finish(wb, inflow, extent, mixing, out_hbm, ob, out_sem):
@@ -400,7 +427,8 @@
             vm((V, J, L, I), f32),
             vm((V, J, L, I), f32),
             vm((V, J, L, I), f32),
-            vm((LAT, 4, I), f32),
+            vm((LAT, Q, I), f32),
+            vm((ROWS, Q, I), f32),
             vm((8, L, I), f32),
             vm((8, L, I), f32),
             vm((V, L, I), f32),
@@ -410,13 +438,18 @@
             vm((LON, 1, I), f32),
             vm((3, LON, I), f32),
             vm((LON, 3, 8, I), f32),
-            vm((LAT, 4, I), f32),
-            vm((LAT, 4, I), f32),
-            vm((LAT, 4, I), f32),
-            vm((LAT, 4, I), f32),
+            vm((ROW, Q, I), f32),
+            vm((ROW, Q, I), f32),
+            vm((Q, I), f32),
+            vm((ROWS, Q, I), f32),
+            vm((Q, I), f32),
+            vm((ROW, Q, I), f32),
+            vm((ROW, Q, I), f32),
             pltpu.SemaphoreType.DMA((10,)),
-            pltpu.SemaphoreType.DMA((5,)),
-            pltpu.SemaphoreType.DMA((6,)),
+            pltpu.SemaphoreType.DMA((4,)),
+            pltpu.SemaphoreType.DMA((4,)),
+            pltpu.SemaphoreType.DMA((ROWS,)),
+            pltpu.SemaphoreType.DMA((ROWS,)),
         ],
         compiler_params=pltpu.CompilerParams(
             collective_id=0, has_side_effects=True, vmem_limit_bytes=48 * 1024 * 1024

time: 35.8 us -> 33.1 us (0.925)
  the two profiles are of different devices: /device:TPU:64 before, /device:TPU:56 now
where the time goes in v4:
time: 33.1 us; the launch traced here: 33 us
  Pallas kernels  32.9 us (99%)
    pallas_call x1, Pallas kernels, shards(): pl.pallas_call(kernel, out_shape=[vm((V, J, L, I), f32), vm((V, L, I), f3...  31.3 us
    pallas_call x1, Pallas kernels, shards(): pl.pallas_call(finish, out_shape=jax.ShapeDtypeStruct((V, L, J, I), f32),...  1.63 us

profile of v4, /device:TPU:56, one launch (start us, length us, event | category | flops | bytes accessed | tf_op | source)
XLA Modules:
  0.0 33.0 jit_solution(2387249143056357031)
XLA Ops:
  0.0 31.3 %shard_map.55 = (f32[2,24,64,128]{3,2,1,0:T(8,128)S(1)}, f32[2,64,128]{2,1,0:T(8,128)S(1)}, f32[2,64,128]{2,1,0:T(8,128)S(1)}, bf16[2,64,192]{2,1,0:T(8,128)(2,1)S(1)}) custom-call(f32[2,64,24,128]{3,2,1,0:T(8,128)} %x_hbm.1, f32[2,24,64]{2,1,0:T(8,128)} %bitcast.1, f32[24,128]{1,0:T(8,128)} %sp_hbm.1, f32[2,64,768]{2,1,0:T(8,128)} %nr_hbm.1, ...), custom_call_target="tpu_custom_call" | custom-call | tf_op jit(solution)/shard_map/pallas_call | solution.py:406
  31.3 1.6 %shard_map.56 = f32[2,64,24,128]{3,2,1,0:T(8,128)} custom-call(f32[2,24,64,128]{3,2,1,0:T(8,128)S(1)} %get-tuple-element.9.wb, f32[2,64,128]{2,1,0:T(8,128)S(1)} %get-tuple-element.10.inflow, f32[2,64,128]{2,1,0:T(8,128)S(1)} %get-tuple-element.11.extent, bf16[2,64,192]{2,1,0:T(8,128)(2,1)S(1)} %get-tuple-element.12.mixing), custom_call_target="tpu_custom_call" | custom-call | tf_op jit(solution)/shard_map/pallas_call | solution.py:458

commit v5 on v4

--- a/solution.py
+++ b/solution.py
@@ -11,6 +11,7 @@
 ROW, ROWS = 4, 8
 MESH = pl.DeviceIdType.MESH
 f32 = jnp.float32
+FAR_ROWS = (4, 3, 5, 2, 6, 1, 7)
 
 
 def lanes(rows):
@@ -322,7 +323,7 @@
     for c in range(1, ROW):
         total = r3[c] + gb[ROW * row + c] * total
     st[...] = total
-    for t in range(1, ROWS):
+    for t in FAR_ROWS:
 
         @pl.when(row + t < ROWS)
         def _():

time: 33.1 us -> 32.8 us (level)
    pallas_call x1, Pallas kernels: 31.3 us -> 30.9 us  [shards(): pl.pallas_call(kernel, out_shape=[vm((V, J, L, I), f32), vm((V, L, I), f3...]
where the time goes in v5:
time: 32.8 us; the launch traced here: 32.6 us
  Pallas kernels  32.6 us (99%)
    pallas_call x1, Pallas kernels, shards(): pl.pallas_call(kernel, out_shape=[vm((V, J, L, I), f32), vm((V, L, I), f3...  30.9 us
    pallas_call x1, Pallas kernels, shards(): pl.pallas_call(finish, out_shape=jax.ShapeDtypeStruct((V, L, J, I), f32),...  1.63 us

profile of v5, /device:TPU:56, one launch (start us, length us, event | category | flops | bytes accessed | tf_op | source)
XLA Modules:
  0.0 32.6 jit_solution(1530664383512765079)
XLA Ops:
  0.0 30.9 %shard_map.55 = (f32[2,24,64,128]{3,2,1,0:T(8,128)S(1)}, f32[2,64,128]{2,1,0:T(8,128)S(1)}, f32[2,64,128]{2,1,0:T(8,128)S(1)}, bf16[2,64,192]{2,1,0:T(8,128)(2,1)S(1)}) custom-call(f32[2,64,24,128]{3,2,1,0:T(8,128)} %x_hbm.1, f32[2,24,64]{2,1,0:T(8,128)} %bitcast.1, f32[24,128]{1,0:T(8,128)} %sp_hbm.1, f32[2,64,768]{2,1,0:T(8,128)} %nr_hbm.1, ...), custom_call_target="tpu_custom_call" | custom-call | tf_op jit(solution)/shard_map/pallas_call | solution.py:407
  31.0 1.6 %shard_map.56 = f32[2,64,24,128]{3,2,1,0:T(8,128)} custom-call(f32[2,24,64,128]{3,2,1,0:T(8,128)S(1)} %get-tuple-element.9.wb, f32[2,64,128]{2,1,0:T(8,128)S(1)} %get-tuple-element.10.inflow, f32[2,64,128]{2,1,0:T(8,128)S(1)} %get-tuple-element.11.extent, bf16[2,64,192]{2,1,0:T(8,128)(2,1)S(1)} %get-tuple-element.12.mixing), custom_call_target="tpu_custom_call" | custom-call | tf_op jit(solution)/shard_map/pallas_call | solution.py:459
